TPU v7x, 256 devices: a whole 4x4x8 slice. The times are simulated.
256 devices in a mesh: img: 32 (over z, x_lo, core), phr: 8 (over x_hi, y).
Axes of the slice: x: 4 (x_hi: 2, x_lo: 2; x = x_hi * 2 + x_lo), y: 4, z: 8, core: 2. Of those that a mesh axis runs over, the one named last changes fastest.
Arguments:
- image_cell_features: bfloat16 [2048, 256, 1152], P(('img', 'phr')), may hold values from -0.29882812 to 0.29882812
- area_rectangle_limits: int32 [24576, 4], P(('img', 'phr')), may hold values from 0 to 16, as said below
- area_shard_index: int32 [24576], replicated, may hold values from 0 to 31, as said below
- caption_described_area: int32 [98304], replicated, may hold values from 0 to 24575, as said below
- caption_embeddings: bfloat16 [98304, 1152], P(('img', 'phr')), may hold values from -6 to 6
- sharpness_multiplier: float32 [1], replicated, may hold values from 20 to 40
- sigmoid_shift_term: float32 [1], replicated, may hold values from -4 to -2
Outputs:
- patch_grad: bfloat16 [2048, 256, 1152], P(('img', 'phr'))
Inputs may be any that keep to these rules, and one draw needn't show every extreme that they name: `area_rectangle_limits`: each row is a box of at least one patch: first row < end row, first column < end column. Region k of a device lies in that device's image k // 12. `area_shard_index`: among the 96 regions of one device at most 7 go to any one shard; in every draw every device sends exactly 7 to some shard. `caption_described_area`: phrase p names a region assigned to shard p // 3072 whenever that shard has any region.
All inputs are finite; a program needn't handle non-finite values.
Results may differ from a plain program's by a relative error of at most 0.01.
Values may be sent and summed in bfloat16 or wider, within the bound.
A program may use at most 64 MiB of HBM per device.

v0:
```python
import jax
import jax.numpy as jnp
from jax import lax
from jax.sharding import PartitionSpec as P

GRID = 16


epsilon = 1e-06


def box_masks(area_rectangle_limits, img_dev, patch_count):
    reg_img = area_rectangle_limits.shape[0] // img_dev
    spot_ids = jnp.arange(patch_count, dtype=jnp.int32)
    patch_row = spot_ids // GRID
    patch_col = spot_ids % GRID
    corners = area_rectangle_limits.reshape(img_dev, reg_img, 4)
    inside = (
        (patch_row >= corners[:, :, 0:1])
        & (patch_row < corners[:, :, 1:2])
        & (patch_col >= corners[:, :, 2:3])
        & (patch_col < corners[:, :, 3:4])
    )
    return inside.astype(jnp.bfloat16)


def ranks_within(shard_ids):
    reg_dev = shard_ids.shape[-1]
    local_ids = jnp.arange(reg_dev, dtype=jnp.int32)
    earlier = local_ids[None, :] < local_ids[:, None]
    same_shard = shard_ids[:, None] == shard_ids[None, :]
    return jnp.sum((same_shard & earlier).astype(jnp.int32), axis=1)


def tile_terms(
    region_unit,
    usable,
    region_col,
    target_slot,
    target_col,
    block_rows,
    sigmoid_stretch_amount,
    offset,
):
    similarity_grid_scores = (
        sigmoid_stretch_amount
        * lax.dot_general(
            region_unit, block_rows, (((1,), (1,)), ((), ())), preferred_element_type=jnp.float32
        )
        + offset
    )
    slot_ids = jnp.arange(region_unit.shape[0], dtype=jnp.int32)
    positive = (target_slot[None, :] == slot_ids[:, None]) & (target_col[None, :] == region_col)
    averaging_coefficient = (
        (jax.nn.sigmoid(similarity_grid_scores) - positive.astype(jnp.float32)) * usable[:, None]
    ).astype(jnp.bfloat16)
    return sigmoid_stretch_amount * jnp.dot(
        averaging_coefficient, block_rows, preferred_element_type=jnp.float32
    )


def shards(
    image_cell_features,
    area_rectangle_limits,
    area_shard_index,
    caption_described_area,
    caption_embeddings,
    sharpness_multiplier,
    sigmoid_shift_term,
):
    n_img = lax.axis_size("img")
    n_phr = lax.axis_size("phr")
    shard_row = lax.axis_index("img")
    column = lax.axis_index("phr")
    img_dev, patch_count, feat_dim = image_cell_features.shape
    reg_dev = area_rectangle_limits.shape[0]
    ph_dev = caption_embeddings.shape[0]
    reg_img = reg_dev // img_dev
    cap_slots = max(2, 5 * reg_dev // (2 * n_img))
    slot_count = n_img * cap_slots
    sigmoid_stretch_amount = sharpness_multiplier[0]
    offset = sigmoid_shift_term[0]
    inside = box_masks(area_rectangle_limits, img_dev, patch_count)
    pooled = jnp.einsum(
        "mrp,mpd->mrd", inside, image_cell_features, preferred_element_type=jnp.float32
    )
    pooled = pooled.reshape(reg_dev, feat_dim).astype(jnp.bfloat16)
    owners = area_shard_index.reshape(n_img, n_phr, reg_dev)
    own_shards = lax.dynamic_index_in_dim(
        lax.dynamic_index_in_dim(owners, shard_row, 0, False), column, 0, False
    )
    own_slot = own_shards * cap_slots + ranks_within(own_shards)
    dispatch = (jnp.arange(slot_count, dtype=jnp.int32)[:, None] == own_slot[None, :]).astype(
        jnp.bfloat16
    )
    outgoing = jnp.dot(dispatch, pooled, preferred_element_type=jnp.float32).astype(jnp.bfloat16)
    arrived = lax.all_to_all(
        outgoing.reshape(n_img, cap_slots, feat_dim), "img", split_axis=0, concat_axis=0, tiled=True
    )
    arrived_f = arrived.reshape(slot_count, feat_dim).astype(jnp.float32)
    inverse = lax.rsqrt(jnp.sum(arrived_f * arrived_f, axis=1, keepdims=True) + epsilon)
    region_unit = (arrived_f * inverse).astype(jnp.bfloat16)
    row_len = n_phr * ph_dev
    named_ids = lax.dynamic_slice_in_dim(caption_described_area, shard_row * row_len, row_len)
    source = named_ids // reg_dev
    local_spot = named_ids % reg_dev
    source_rows = jnp.take(area_shard_index.reshape(n_img * n_phr, reg_dev), source, axis=0)
    named_shard = jnp.take(area_shard_index, named_ids)
    before = jnp.arange(reg_dev, dtype=jnp.int32)[None, :] < local_spot[:, None]
    named_rank = jnp.sum(((source_rows == named_shard[:, None]) & before).astype(jnp.int32), axis=1)
    target_slot = jnp.where(named_shard == shard_row, source // n_phr * cap_slots + named_rank, -1)
    target_col = source % n_phr
    phrase_f = caption_embeddings.astype(jnp.float32)
    phrase_unit = (
        phrase_f * lax.rsqrt(jnp.sum(phrase_f * phrase_f, axis=1, keepdims=True) + epsilon)
    ).astype(jnp.bfloat16)
    row_phrases = lax.all_gather(phrase_unit, "phr", axis=0, tiled=True)
    sources = lax.dynamic_index_in_dim(owners, column, 1, False)
    arrived_count = jnp.sum((sources == shard_row).astype(jnp.int32), axis=1)
    slot_live = jnp.arange(cap_slots, dtype=jnp.int32)[None, :] < arrived_count[:, None]
    pull_sum = tile_terms(
        region_unit,
        slot_live.reshape(slot_count).astype(jnp.float32),
        column,
        target_slot,
        target_col,
        row_phrases,
        sigmoid_stretch_amount,
        offset,
    )
    radial = jnp.sum(arrived_f * pull_sum, axis=1, keepdims=True)
    region_pull = inverse * pull_sum - inverse**3 * radial * arrived_f
    returned = lax.all_to_all(
        region_pull.reshape(n_img, cap_slots, feat_dim).astype(jnp.bfloat16),
        "img",
        split_axis=0,
        concat_axis=0,
        tiled=True,
    ).astype(jnp.float32)
    returned = returned.reshape(slot_count, feat_dim)
    region_grad = jnp.take(returned, own_slot, axis=0).reshape(img_dev, reg_img, feat_dim)
    upper_part = region_grad.astype(jnp.bfloat16)
    lower_part = (region_grad - upper_part.astype(jnp.float32)).astype(jnp.bfloat16)
    patch_grad = (
        jnp.einsum("mrp,mrd->mpd", inside, upper_part, preferred_element_type=jnp.float32)
        + jnp.einsum("mrp,mrd->mpd", inside, lower_part, preferred_element_type=jnp.float32)
    ).astype(jnp.bfloat16)
    return patch_grad


def solution(mesh):
    return jax.shard_map(
        shards,
        mesh=mesh,
        in_specs=(
            P(("img", "phr"), None, None),
            P(("img", "phr"), None),
            P(),
            P(),
            P(("img", "phr"), None),
            P(),
            P(),
        ),
        out_specs=P(("img", "phr"), None, None),
        check_vma=False,
    )
```

profile of v0, /device:TPU:1, one launch (start us, length us, event | category | flops | bytes accessed | tf_op | source)
XLA Modules:
  0.0 170.4 jit_solution(14387672347590595404)
XLA Ops:
  6.5 1.5 fusion.9
  8.0 2.3 %fusion.10 = bf16[384,1152]{1,0:T(8,128)(2,1)} fusion(bf16[384,1152]{1,0:T(8,128)(2,1)} %param.11, f32[384]{0:T(512)S(1)} %add_rsqrt_fusion.1), kind=kLoop, calls=%fused_computation.21 | loop fusion | flops 1327104 | bytes 1771008 | tf_op jit(solution)/shard_map/convert_element_type | solution.py:116
  10.5 3.1 %convolution_convert_fusion.1 = bf16[8,12,1152]{2,1,0:T(8,128)(2,1)S(1)} fusion(bf16[8,256,1152]{2,1,0:T(8,128)(2,1)} %param.7, s32[8,12]{1,0:T(8,128)S(1)} %get-tuple-element.13, s32[8,12]{1,0:T(8,128)S(1)} %get-tuple-element.14, s32[256]{0:T(256)S(1)} %get-tuple-element.18, s32[8,12]{1,0:T(8,128)S(1)} %get-tuple-element.15, ...), kind=kOutput, calls=%fused_computation.17 | convolution fusion | flops 56905728 | bytes 4943360 | tf_op jit(solution)/shard_map/mrp,mpd->mrd/dot_general | solution.py:84
  13.9 0.3 convolution_convert_fusion
  14.2 1.0 reshape.175
  15.2 11.1 %all-to-all-start = ((bf16[32,7,1152]{2,1,0:T(8,128)(2,1)}), bf16[32,7,1152]{2,1,0:T(8,128)(2,1)S(1)}, u32[]{:S(2)}, u32[]{:S(2)}) async-start(bf16[32,7,1152]{2,1,0:T(8,128)(2,1)} %reshape.175), calls=%async_computation | async-start | bytes 1179648 | tf_op jit(solution)/shard_map/all_to_all | solution.py:97
  27.7 0.7 fusion.30
  28.4 17.4 %gather_fusion = s32[3072]{0:T(1024)S(1)} fusion(s32[24576]{0:T(1024)S(1)} %copy-done, s32[3072]{0:T(1024)S(1)} %fusion.30), kind=kCustom, calls=%fused_computation | custom fusion | bytes 36864 | tf_op jit(solution)/shard_map/jit(_take)/gather | solution.py:108
  45.8 0.7 fusion.21
  46.7 0.7 and_select_fusion
  47.4 8.1 %gather_fusion.1 = s32[3072,96]{1,0:T(8,128)S(1)} fusion(s32[256,96]{1,0:T(8,128)S(1)} %reshape.176, s32[3072]{0:T(1024)S(1)} %get-tuple-element.10), kind=kCustom, calls=%fused_computation.1 | custom fusion | bytes 2371584 | tf_op jit(solution)/shard_map/jit(_take)/gather | solution.py:107
  55.5 0.7 fusion.26
  56.3 3.0 %convert_reduce_fusion = s32[3072]{0:T(1024)S(1)} fusion(s32[3072,96]{1,0:T(8,128)S(1)} %gather_fusion.1, s32[3072]{0:T(1024)S(1)} %get-tuple-element.11, s32[3072]{0:T(1024)S(1)} %get-tuple-element.9, pred[3072]{0:T(1024)(128)(4,1)S(1)} %get-tuple-element.8), kind=kLoop, calls=%fused_computation.22 | loop fusion | flops 1766400 | bytes 1219584 | tf_op jit(solution)/shard_map/reduce_sum | solution.py:110
  59.3 0.7 fusion.25
  60.0 0.2 multiply_reduce_fusion
  60.5 59.3 %all-gather.2.cloned.1.call-done = bf16[3072,1152]{1,0:T(8,128)(2,1)} async-done(((bf16[384,1152]{1,0:T(8,128)(2,1)}), bf16[3072,1152]{1,0:T(8,128)(2,1)}) %all-gather.2.cloned.1.call-update) | async-done | bytes 7077904 | tf_op jit(solution)/shard_map/all_gather | solution.py:117
  119.9 9.5 %multiply_reduce_fusion.1 = (f32[224]{0:T(256)S(1)}, f32[224,1152]{1,0:T(8,128)S(1)}) fusion(f32[224,1152]{1,0:T(8,128)S(1)} %reshape.179, bf16[3072,1152]{1,0:T(8,128)(2,1)} %all-gather.2.cloned.1.call-done, f32[224]{0:T(256)S(1)} %reshape.180, s32[3072]{0:T(1024)S(1)} %fusion.25, f32[]{:T(128)} %bitcast.27, f32[]{:T(128)} %bitcast.26, ...), kind=kOutput, calls=%fused_computation.28 | convolution fusion | flops 3179753216 | bytes 9160328 | tf_op jit(solution)/shard_map/dot_general | solution.py:57
  129.3 0.2 subtract_convert_fusion
  129.5 1.0 convert_element_type.91
  130.5 8.3 %all-to-all-start.1 = ((bf16[32,7,1152]{2,1,0:T(8,128)(2,1)}), bf16[32,7,1152]{2,1,0:T(8,128)(2,1)S(1)}, u32[]{:S(2)}, u32[]{:S(2)}) async-start(bf16[32,7,1152]{2,1,0:T(8,128)(2,1)} %convert_element_type.91), calls=%async_computation.1 | async-start | bytes 1179648 | tf_op jit(solution)/shard_map/all_to_all | solution.py:133
  139.0 18.4 %all-to-all-done.1 = bf16[32,7,1152]{2,1,0:T(8,128)(2,1)S(1)} async-done(((bf16[32,7,1152]{2,1,0:T(8,128)(2,1)}), bf16[32,7,1152]{2,1,0:T(8,128)(2,1)S(1)}, u32[]{:S(2)}, u32[]{:S(2)}) %all-to-all-start.1) | async-done | bytes 516128 | tf_op jit(solution)/shard_map/all_to_all | solution.py:133
  157.5 0.8 gather_fusion.2
  158.4 1.5 fusion.14
  159.9 3.7 %add_convert_fusion = bf16[8,256,1152]{2,1,0:T(8,128)(2,1)} fusion(f32[8,256,1152]{2,1,0:T(8,128)S(1)} %fusion.14, f32[8,12,1152]{2,1,0:T(8,128)S(1)} %gather.17, pred[8,12]{1,0:T(8,128)(4,1)S(1)} %compare_and_fusion.2, s32[8,12]{1,0:T(8,128)S(1)} %get-tuple-element.13, s32[8,12]{1,0:T(8,128)S(1)} %get-tuple-element.14, s32[256]{0:T(256)S(1)} %get-tuple-element.18, ...), kind=kOutput, calls=%fused_computation.3 | convolution fusion | flops 62066688 | bytes 14601824 | tf_op jit(solution)/shard_map/mrp,mrd->mpd/dot_general | solution.py:146
  (30 shorter events, 1.4 us)
Async XLA Ops:
  6.5 3.8 %copy-start.1 = (s32[96,4]{0,1:T(4,128)S(1)}, s32[96,4]{0,1:T(4,128)}, u32[]{:S(2)}) copy-start(s32[96,4]{0,1:T(4,128)} %param.8) | copy-start | bytes 4612
  6.5 3.9 %copy-start = (s32[24576]{0:T(1024)S(1)}, s32[24576]{0:T(1024)}, u32[]{:S(2)}) copy-start(s32[24576]{0:T(1024)} %param.9) | copy-start | bytes 294916
  6.5 113.3 %all-gather.2.cloned.1.call-start = ((), (), s32[]{:S(2)}) async-start(), calls=%async_computation.2 | async-start | bytes 7962624 | tf_op jit(solution)/shard_map/all_gather | solution.py:117
  15.2 44.8 %all-to-all-start = ((bf16[32,7,1152]{2,1,0:T(8,128)(2,1)}), bf16[32,7,1152]{2,1,0:T(8,128)(2,1)S(1)}, u32[]{:S(2)}, u32[]{:S(2)}) async-start(bf16[32,7,1152]{2,1,0:T(8,128)(2,1)} %reshape.175), calls=%async_computation | async-start | bytes 1179648 | tf_op jit(solution)/shard_map/all_to_all | solution.py:97
  130.5 26.8 %all-to-all-start.1 = ((bf16[32,7,1152]{2,1,0:T(8,128)(2,1)}), bf16[32,7,1152]{2,1,0:T(8,128)(2,1)S(1)}, u32[]{:S(2)}, u32[]{:S(2)}) async-start(bf16[32,7,1152]{2,1,0:T(8,128)(2,1)} %convert_element_type.91), calls=%async_computation.1 | async-start | bytes 1179648 | tf_op jit(solution)/shard_map/all_to_all | solution.py:133
Sparse Core Ops, SparseCore 0:
  10.4 109.3 all-gather.1
where the time goes:
time: 171 us; the launch traced here: 170 us
  waiting for transfers between devices  77.7 us (45%)
  local copies, waits for them, and re-layouts  29.3 us (17%)
  starting transfers between devices  19.3 us (11%)
  matrix products  18.1 us (11%)
  between operations  14.9 us (9%)
  other arithmetic  11.1 us (6%)
    all_gather x1, waiting for transfers between devices, shards(): row_phrases = lax.all_gather(phrase_unit, 'phr', axis=0, tiled=True)  59.3 us
    all_to_all x1, waiting for transfers between devices, shards(): lax.all_to_all(region_pull.reshape(n_img, cap_slots, feat_dim).astype(jnp...  18.4 us
    gather x1, local copies, waits for them, and re-layouts, shards(): named_shard = jnp.take(area_shard_index, named_ids)  17.4 us
    all_to_all x1, starting transfers between devices, shards(): lax.all_to_all(outgoing.reshape(n_img, cap_slots, feat_dim), 'img', split...  11.1 us
    dot_general x1, matrix products, tile_terms(): jnp.dot(averaging_coefficient, block_rows, preferred_element_type=jnp.flo...  9.45 us
    all_to_all x1, starting transfers between devices, shards(): lax.all_to_all(region_pull.reshape(n_img, cap_slots, feat_dim).astype(jnp...  8.26 us
    gather x1, local copies, waits for them, and re-layouts, shards(): jnp.take(area_shard_index.reshape(n_img * n_phr, reg_dev), source, axis=0)  8.12 us
    dot_general x1, matrix products, shards(): jnp.einsum('mrp,mrd->mpd', inside, lower_part, preferred_element_type=jnp...  3.72 us
  transfers between devices with their start and end apart: 3, of which 2 were waited for; matrix products, arithmetic and copies ran while one was open for 22% of the time, Pallas kernels for 0%

commit v1 on v0

v1 whole, which is shorter than its diff:
```python
import jax
import jax.numpy as jnp
from jax import lax
from jax.experimental import pallas as pl
from jax.experimental.pallas import tpu as pltpu
from jax.sharding import PartitionSpec as P

MESH = pl.DeviceIdType.MESH
GRID = 16
NZ, NX, NY = 8, 4, 4
SLOT = 8
EPS = 1e-06
BF16, F32, I32 = jnp.bfloat16, jnp.float32, jnp.int32

ORDER = (4, 3, 5, 2, 6, 1, 7, 0)
PLACE = {rel: k for k, rel in enumerate(ORDER)}


def place():
    img, phr = lax.axis_index("img"), lax.axis_index("phr")
    return img // 4, (phr // 4) * 2 + (img // 2) % 2, phr % 4, img % 2


def device_at(z, x, y, c):
    z, x, y, c = lax.rem(z, NZ), lax.rem(x, NX), lax.rem(y, NY), lax.rem(c, 2)
    return ((z * 2 + lax.rem(x, 2)) * 2 + c, (x // 2) * 4 + y)


def iota(shape, dim):
    return lax.broadcasted_iota(I32, shape, dim)


def dot(a, b):
    return jnp.dot(a, b, preferred_element_type=F32)


def exchange_kernel(
    sharp_ref,
    shift_ref,
    limits_ref,
    shard_ref,
    named_hbm,
    phrase_hbm,
    feature_hbm,
    back_ref,
    spread_ref,
    feature,
    raw,
    named,
    phrases,
    pool,
    z_out,
    z_in,
    x_out,
    x_in,
    unit,
    ids,
    inverse,
    total,
    p_out,
    p_in,
    s_out,
    in_sem,
    feature_sem,
    y_send,
    y_recv,
    zf_send,
    zf_recv,
    xf_send,
    xf_recv,
    xr_send,
    xr_recv,
    zr_send,
    zr_recv,
):
    z, x, y, c = place()
    me_img, me_phr = lax.axis_index("img"), lax.axis_index("phr")
    shard = me_img
    reg_dev = limits_ref.shape[0]
    n_dev = shard_ref.shape[0]
    ph_dev = raw.shape[0]
    half = ph_dev // 2
    reg_img = 12
    patches = GRID * GRID
    n_feature = feature_sem.shape[0]
    chunk = feature.shape[0] // n_feature

    def remote(src, dst, send, recv, dz=0, dx=0, dy=0, dc=0):
        return pltpu.make_async_remote_copy(
            src_ref=src,
            dst_ref=dst,
            send_sem=send,
            recv_sem=recv,
            device_id=device_at(z + dz % NZ, x + dx % NX, y + dy % NY, c + dc),
            device_id_type=MESH,
        )

    phrase_copy = pltpu.make_async_copy(phrase_hbm, raw, in_sem.at[0])
    phrase_copy.start()
    feature_copies = []
    for i in range(n_feature):
        rows = pl.ds(i * chunk, chunk)
        copy = pltpu.make_async_copy(feature_hbm.at[rows], feature.at[rows], feature_sem.at[i])
        copy.start()
        feature_copies.append(copy)
    named_copy = pltpu.make_async_copy(named_hbm.at[pl.ds(shard * 24, 24)], named, in_sem.at[1])
    named_copy.start()

    barrier = pltpu.get_barrier_semaphore()
    partners = [(dz, 0, 0, dc) for dz in range(NZ) for dc in range(2) if (dz, dc) != (0, 0)]
    partners += [(0, dx, 0, 0) for dx in range(1, NX)] + [(0, 0, 1, 0), (0, 0, 3, 0)]
    for dz, dx, dy, dc in partners:
        pl.semaphore_signal(
            barrier, inc=1, device_id=device_at(z + dz, x + dx, y + dy, c + dc), device_id_type=MESH
        )

    phrase_copy.wait()
    for i in range(0, ph_dev, 64):
        rows = pl.ds(i, 64)
        own = raw[rows].astype(F32)
        scale = lax.rsqrt(jnp.sum(own * own, axis=1, keepdims=True) + EPS)
        phrases[rows] = (own * scale).astype(BF16)
    pl.semaphore_wait(barrier, len(partners))

    def part(block, which):
        return phrases.at[pl.ds(block * ph_dev + which * half, half)]

    def ring(index, src, dst, dy):
        return remote(src, dst, y_send.at[index], y_recv.at[index], dy=dy)

    ring_copies = [
        ring(0, part(0, 0), part(1, 0), 1),
        ring(1, part(0, 1), part(2, 1), -1),
        ring(2, part(0, 1), part(1, 1), 1),
        ring(3, part(0, 0), part(2, 0), -1),
        ring(4, part(1, 0), part(3, 0), 1),
        ring(5, part(2, 1), part(3, 1), -1),
    ]
    for copy in ring_copies[:4]:
        copy.start()

    own = shard_ref[pl.ds(me_img * 8 + me_phr, 1), :]
    member = (iota((32, reg_dev), 0) == own).astype(F32)
    earlier = (iota((reg_dev, reg_dev), 0) < iota((reg_dev, reg_dev), 1)).astype(BF16)
    rank = jnp.sum(member * dot(member.astype(BF16), earlier), axis=0, keepdims=True).astype(I32)
    parity = lax.rem(x, 2)
    to_z = ((own >> 2) - z + NZ) & (NZ - 1)
    to_c = jnp.where((own & 1) == c, 0, 1)
    to_x = jnp.where(((own >> 1) & 1) == parity, 0, 1)
    goes = ((to_z * 2 + to_c) * 2 + to_x) * SLOT + rank
    slots = NZ * 4 * SLOT
    dispatch = (iota((slots, reg_dev), 0) == goes).astype(BF16)

    spot = iota((reg_dev, patches), 1)
    spot_row, spot_col = spot >> 4, spot & 15
    inside = (
        (spot_row >= limits_ref[:, 0:1])
        & (spot_row < limits_ref[:, 1:2])
        & (spot_col >= limits_ref[:, 2:3])
        & (spot_col < limits_ref[:, 3:4])
    )
    region = iota((reg_dev, patches), 0)
    images = chunk // patches
    for i in range(n_feature):
        feature_copies[i].wait()
        mask = jnp.concatenate(
            [
                (
                    inside
                    & (region >= (i * images + m) * reg_img)
                    & (region < (i * images + m + 1) * reg_img)
                ).astype(F32)
                for m in range(images)
            ],
            axis=1,
        ).astype(BF16)
        term = dot(mask, feature[pl.ds(i * chunk, chunk)])
        pool[...] = term if i == 0 else pool[...] + term
    z_out[...] = dot(dispatch, pool[...].astype(BF16)).astype(BF16)

    def block(ref, index):
        return ref.at[pl.ds(index * 2 * SLOT, 2 * SLOT)]

    z_copies = {}
    for dz in ORDER:
        for dc in range(2):
            if (dz, dc) == (0, 0):
                continue
            there = (NZ - dz) % NZ
            copy = remote(
                block(z_out, dz * 2 + dc),
                block(z_in, there * 2 + dc),
                zf_send.at[dz, dc],
                zf_recv.at[there, dc],
                dz=dz,
                dc=dc,
            )
            copy.start()
            z_copies[dz, dc] = copy

    live = 4 * NZ * 2 * SLOT
    member_all = (shard_ref[...] == shard).astype(BF16)
    rank_all = dot(member_all, earlier).astype(BF16)
    slot = iota((live, n_dev), 0)
    k, xr, dc_, r_ = slot >> 6, (slot >> 4) & 3, (slot >> 3) & 1, slot & 7
    rel = jnp.zeros_like(k)
    for rel_z, at in PLACE.items():
        rel = jnp.where(k == at, rel_z, rel)
    from_z = (z + rel) & (NZ - 1)
    from_x = (x + xr) & (NX - 1)
    from_c = (c + dc_) & 1
    device = ((from_z * 2 + (from_x & 1)) * 2 + from_c) * 8 + (from_x >> 1) * 4 + y
    pick = (iota((live, n_dev), 1) == device).astype(BF16)
    member_slot = dot(pick, member_all)
    rank_slot = dot(pick, rank_all)
    wanted = r_[:, :reg_dev].astype(F32)
    local = (iota((live, reg_dev), 1) + 1).astype(F32)
    held = jnp.sum(
        jnp.where(rank_slot == wanted, member_slot * local, 0.0), axis=1, keepdims=True
    ).astype(I32)
    ids[...] = jnp.where(held > 0, device[:, :128] * reg_dev + held - 1, -1)

    same = iota((reg_dev, reg_dev), 0) == iota((reg_dev, reg_dev), 1)
    goes_column = jnp.sum(
        jnp.where(same, goes.astype(F32), 0.0), axis=1, keepdims=True
    ).astype(I32)
    collect = (iota((reg_dev, slots), 1) == goes_column).astype(BF16)
    spot = iota((patches, reg_dev), 0)
    spot_row, spot_col = spot >> 4, spot & 15
    limit = [
        jnp.sum(
            jnp.where(same, limits_ref[:, j : j + 1].astype(F32), 0.0), axis=0, keepdims=True
        ).astype(I32)
        for j in range(4)
    ]
    inside = (
        (spot_row >= limit[0])
        & (spot_row < limit[1])
        & (spot_col >= limit[2])
        & (spot_col < limit[3])
    )
    region = iota((patches, reg_dev), 1)
    for m in range(reg_dev // reg_img):
        mask = (inside & (region >= m * reg_img) & (region < (m + 1) * reg_img)).astype(BF16)
        spread_ref[pl.ds(m * patches, patches)] = dot(mask, collect).astype(BF16)

    ring_copies[0].wait_recv()
    ring_copies[4].start()
    ring_copies[1].wait_recv()
    ring_copies[5].start()

    x_copies = {}
    for at, rel_z in enumerate(ORDER):
        sides = []
        for dc in range(2):
            if (rel_z, dc) == (0, 0):
                got = block(z_out, 0)
            else:
                got = block(z_in, rel_z * 2 + dc)
                z_copies[(NZ - rel_z) % NZ, dc].wait_recv()
            sides.append(got[...].astype(F32))
        near, far = [
            jnp.concatenate(
                [side[p * SLOT : (p + 1) * SLOT] for side in sides], axis=0
            ).astype(BF16)
            for p in range(2)
        ]
        block(x_in, at * 4)[...] = near
        block(x_out, at * 2)[...] = near
        block(x_out, at * 2 + 1)[...] = far
        for dx in (2, 1, 3):
            there = NX - dx
            copy = remote(
                block(x_out, at * 2 + dx % 2),
                block(x_in, at * 4 + there),
                xf_send.at[at, dx - 1],
                xf_recv.at[at, there - 1],
                dx=dx,
            )
            copy.start()
            x_copies[at, dx] = copy

    named_copy.wait()
    sharp, shift = sharp_ref[0], shift_ref[0]
    for at in range(NZ):
        for dx in (2, 1, 3):
            x_copies[at, dx].wait_recv()
        rows = pl.ds(at * 64, 64)
        arrived = x_in[rows].astype(F32)
        inv = lax.rsqrt(jnp.sum(arrived * arrived, axis=1, keepdims=True) + EPS)
        inverse[rows] = jnp.broadcast_to(inv, (64, 128))
        unit[rows] = (arrived * inv).astype(BF16)

    def pairs(rows, count, which, dy):
        them = phrases[pl.ds(which * ph_dev, ph_dev)]
        scores = lax.dot_general(
            unit[rows], them, (((1,), (1,)), ((), ())), preferred_element_type=F32
        )
        first = (me_phr // 4) * 12 + lax.rem(y + dy, NY) * 3
        mine = ids[rows]
        weights = []
        for j in range(ph_dev // 128):
            logits = sharp * scores[:, j * 128 : (j + 1) * 128] + shift
            positive = (mine == named[pl.ds(first + j, 1), :]).astype(F32)
            weights.append((jax.nn.sigmoid(logits) - positive).astype(BF16))
        return dot(jnp.concatenate(weights, axis=1), them)

    everything = pl.ds(0, live)
    total[...] = pairs(everything, live, 0, 0)
    ring_copies[2].wait_recv()
    total[...] += pairs(everything, live, 1, 3)
    ring_copies[3].wait_recv()
    total[...] += pairs(everything, live, 2, 1)
    ring_copies[4].wait_recv()
    ring_copies[5].wait_recv()
    r_copies = {}
    for part_rows in range(2):
        rows = pl.ds(part_rows * (live // 2), live // 2)
        total[rows] += pairs(rows, live // 2, 3, 2)
        for at in range(part_rows * 4, part_rows * 4 + 4):
            rows = pl.ds(at * 64, 64)
            pull = sharp * total[rows]
            arrived = x_in[rows].astype(F32)
            inv = inverse[rows][:, 0:1]
            radial = jnp.sum(arrived * pull, axis=1, keepdims=True)
            p_out[rows] = (inv * pull - (inv * inv * inv * radial) * arrived).astype(BF16)
            for dx in (2, 1, 3):
                there = NX - dx
                copy = remote(
                    block(p_out, at * 4 + dx),
                    block(p_in, at * 4 + there),
                    xr_send.at[at, dx - 1],
                    xr_recv.at[at, there - 1],
                    dx=dx,
                )
                copy.start()
                r_copies[at, dx] = copy

    home_copies = {}
    for at, rel_z in enumerate(ORDER):
        for dx in (2, 1, 3):
            r_copies[at, dx].wait_recv()
        near = block(p_out, at * 4)[...].astype(F32) + block(p_in, at * 4 + 2)[...].astype(F32)
        far = block(p_in, at * 4 + 1)[...].astype(F32) + block(p_in, at * 4 + 3)[...].astype(F32)
        there = (NZ - rel_z) % NZ
        for dc in range(2):
            rows = slice(dc * SLOT, (dc + 1) * SLOT)
            both = jnp.concatenate([near[rows], far[rows]], axis=0).astype(BF16)
            if (rel_z, dc) == (0, 0):
                block(back_ref, 0)[...] = both
                continue
            block(s_out, rel_z * 2 + dc)[...] = both
            copy = remote(
                block(s_out, rel_z * 2 + dc),
                block(back_ref, there * 2 + dc),
                zr_send.at[rel_z, dc],
                zr_recv.at[there, dc],
                dz=rel_z,
                dc=dc,
            )
            copy.start()
            home_copies[rel_z, dc] = copy

    for copy in home_copies.values():
        copy.wait_recv()
    for copies in (ring_copies, z_copies.values(), x_copies.values(), r_copies.values(), home_copies.values()):
        for copy in copies:
            copy.wait_send()


def spread_kernel(spread_ref, back_ref, out_ref):
    out_ref[0] = dot(spread_ref[...], back_ref[...]).astype(BF16)


def shards(features, limits, shard_index, named, phrases, sharpness, shift):
    images, patches, width = features.shape
    reg_dev, ph_dev = limits.shape[0], phrases.shape[0]
    slots = NZ * 4 * SLOT
    live = slots * 2
    vmem = pl.BlockSpec(memory_space=pltpu.VMEM)
    smem = pl.BlockSpec(memory_space=pltpu.SMEM)
    anywhere = pl.BlockSpec(memory_space=pl.ANY)
    dma = pltpu.SemaphoreType.DMA
    back, spread = pl.pallas_call(
        exchange_kernel,
        out_shape=(
            jax.ShapeDtypeStruct((slots, width), BF16),
            jax.ShapeDtypeStruct((images * patches, slots), BF16),
        ),
        in_specs=[smem, smem, vmem, vmem, anywhere, anywhere, anywhere],
        out_specs=(vmem, vmem),
        scratch_shapes=[
            pltpu.VMEM((images * patches, width), BF16),
            pltpu.VMEM((ph_dev, width), BF16),
            pltpu.VMEM((24, 128), I32),
            pltpu.VMEM((NY * ph_dev, width), BF16),
            pltpu.VMEM((reg_dev, width), F32),
            pltpu.VMEM((slots, width), BF16),
            pltpu.VMEM((slots, width), BF16),
            pltpu.VMEM((slots, width), BF16),
            pltpu.VMEM((live, width), BF16),
            pltpu.VMEM((live, width), BF16),
            pltpu.VMEM((live, 128), I32),
            pltpu.VMEM((live, 128), F32),
            pltpu.VMEM((live, width), F32),
            pltpu.VMEM((live, width), BF16),
            pltpu.VMEM((live, width), BF16),
            pltpu.VMEM((slots, width), BF16),
            dma((2,)),
            dma((4,)),
            dma((6,)),
            dma((6,)),
            dma((NZ, 2)),
            dma((NZ, 2)),
            dma((NZ, 3)),
            dma((NZ, 3)),
            dma((NZ, 3)),
            dma((NZ, 3)),
            dma((NZ, 2)),
            dma((NZ, 2)),
        ],
        compiler_params=pltpu.CompilerParams(
            collective_id=0, has_side_effects=True, vmem_limit_bytes=50 * 2**20
        ),
    )(
        sharpness,
        shift,
        limits,
        shard_index.reshape(-1, reg_dev),
        named.reshape(-1, 128),
        phrases,
        features.reshape(images * patches, width),
    )
    return pl.pallas_call(
        spread_kernel,
        grid=(images,),
        out_shape=jax.ShapeDtypeStruct((images, patches, width), BF16),
        in_specs=[
            pl.BlockSpec((patches, slots), lambda m: (m, 0)),
            pl.BlockSpec((slots, width), lambda m: (0, 0)),
        ],
        out_specs=pl.BlockSpec((1, patches, width), lambda m: (m, 0, 0)),
    )(spread, back)


def solution(mesh):
    return jax.shard_map(
        shards,
        mesh=mesh,
        in_specs=(
            P(("img", "phr"), None, None),
            P(("img", "phr"), None),
            P(),
            P(),
            P(("img", "phr"), None),
            P(),
            P(),
        ),
        out_specs=P(("img", "phr"), None, None),
        check_vma=False,
    )
```

time: 171 us -> 78.5 us (0.46)
  waiting for transfers between devices: 77.7 us -> 0 us
  Pallas kernels: 0 us -> 71.1 us
  local copies, waits for them, and re-layouts: 29.3 us -> 5.7 us
  starting transfers between devices: 19.3 us -> 0 us
  matrix products: 18.1 us -> 0 us
  between operations: 14.9 us -> 1.33 us
  other arithmetic: 11.1 us -> 0 us
    pallas_call x0 -> x2, Pallas kernels: none -> 71.1 us  [the longest x1 63.8 us: shards(): pl.pallas_call(exchange_kernel, out_shape=(jax.ShapeDtypeStruct((slots, w...]
    all_gather x1 -> x0, waiting for transfers between devices: 59.3 us -> none  [shards(): row_phrases = lax.all_gather(phrase_unit, 'phr', axis=0, tiled=True)]
    gather x4 -> x0, local copies, waits for them, and re-layouts: 26.4 us -> none  [the longest x1 17.4 us: shards(): named_shard = jnp.take(area_shard_index, named_ids)]
    all_to_all x2 -> x0, starting transfers between devices: 19.3 us -> none  [the longest x1 11.1 us: shards(): lax.all_to_all(outgoing.reshape(n_img, cap_slots, feat_dim), 'img', split...]
    all_to_all x2 -> x0, waiting for transfers between devices: 18.4 us -> none  [the longest x1 18.4 us: shards(): lax.all_to_all(region_pull.reshape(n_img, cap_slots, feat_dim).astype(jnp...]
    dot_general x5 -> x0, matrix products: 18.1 us -> none  [the longest x1 9.45 us: tile_terms(): jnp.dot(averaging_coefficient, block_rows, preferred_element_type=jnp.flo...]
    reduce_sum x5 -> x0, other arithmetic: 5.52 us -> none  [the longest x1 2.98 us: shards(): jnp.sum(((source_rows == named_shard[:, None]) & before).astype(jnp.int32...]
    unnamed x4 -> x9, local copies, waits for them, and re-layouts: 0.01 us -> 4.72 us
  transfers between devices with their start and end apart: 3 -> 0, of which waited for: 2 -> 0; matrix products, arithmetic and copies ran while one was open for 22% -> 0% of each run, Pallas kernels for 0% -> 0%
where the time goes in v1:
time: 78.5 us; the launch traced here: 78.2 us
  Pallas kernels  71.1 us (91%)
  local copies, waits for them, and re-layouts  5.7 us (7%)
  between operations  1.33 us (2%)
    pallas_call x1, Pallas kernels, shards(): pl.pallas_call(exchange_kernel, out_shape=(jax.ShapeDtypeStruct((slots, w...  63.8 us
    pallas_call x1, Pallas kernels, shards(): pl.pallas_call(spread_kernel, grid=(images,), out_shape=jax.ShapeDtypeStr...  7.35 us
    unnamed x9, local copies, waits for them, and re-layouts  4.72 us

profile of v1, /device:TPU:1, one launch (start us, length us, event | category | flops | bytes accessed | tf_op | source)
XLA Modules:
  0.0 78.2 jit_solution(9307444713492476451)
XLA Ops:
  1.3 0.8 copy.9.limits_ref
  2.1 1.0 %reshape.9.shard_ref = s32[256,96]{1,0:T(8,128)S(1)} reshape(s32[24576]{0:T(1024)} %param.9) | data formatting | bytes 196608 | tf_op jit(solution)/shard_map/reshape | solution.py:429
  3.1 0.0 copy-start.1
  3.1 1.2 %copy-done.1 = bf16[384,1152]{1,0:T(8,128)(2,1)S(1)} copy-done((bf16[384,1152]{1,0:T(8,128)(2,1)S(1)}, bf16[384,1152]{1,0:T(8,128)(2,1)}, u32[]{:S(2)}) %copy-start.1) | copy-done | bytes 884760
  4.2 0.0 copy-start.3
  4.2 1.0 %copy-done.3 = s32[98304]{0:T(1024)S(1)} copy-done((s32[98304]{0:T(1024)S(1)}, s32[98304]{0:T(1024)}, u32[]{:S(2)}) %copy-start.3) | copy-done | bytes 393240
  5.2 63.8 %shard_map.73 = (bf16[256,1152]{1,0:T(8,128)(2,1)S(1)}, bf16[2048,256]{1,0:T(8,128)(2,1)S(1)}) custom-call(f32[1]{0:T(128)S(6)} %copy.10.sharp_ref, f32[1]{0:T(128)S(6)} %copy.11.shift_ref, s32[96,4]{1,0:T(8,128)S(1)} %copy.9.limits_ref, s32[256,96]{1,0:T(8,128)S(1)} %reshape.9.shard_ref, s32[768,128]{1,0:T(8,128)S(1)} %bitcast.2, ...), custom_call_target="tpu_custom_call" | custom-call | tf_op jit(solution)/shard_map/pallas_call | solution.py:384
  69.0 0.0 copy-start
  69.0 1.0 %copy-done = bf16[2048,256]{1,0:T(8,128)(2,1)} copy-done((bf16[2048,256]{1,0:T(8,128)(2,1)}, bf16[2048,256]{1,0:T(8,128)(2,1)S(1)}, u32[]{:S(2)}) %copy-start) | copy-done | bytes 1048600
  70.0 0.0 copy-start.2
  70.0 0.8 %copy-done.2 = bf16[256,1152]{1,0:T(8,128)(2,1)} copy-done((bf16[256,1152]{1,0:T(8,128)(2,1)}, bf16[256,1152]{1,0:T(8,128)(2,1)S(1)}, u32[]{:S(2)}) %copy-start.2) | copy-done | bytes 589848
  70.8 7.4 %shard_map.74 = bf16[8,256,1152]{2,1,0:T(8,128)(2,1)} custom-call(bf16[2048,256]{1,0:T(8,128)(2,1)} %copy-done, bf16[256,1152]{1,0:T(8,128)(2,1)} %copy-done.2), custom_call_target="tpu_custom_call" | custom-call | tf_op jit(solution)/shard_map/pallas_call | solution.py:434
Async XLA Ops:
  3.1 1.2 %copy-start.1 = (bf16[384,1152]{1,0:T(8,128)(2,1)S(1)}, bf16[384,1152]{1,0:T(8,128)(2,1)}, u32[]{:S(2)}) copy-start(bf16[384,1152]{1,0:T(8,128)(2,1)} %phrase_hbm.1) | copy-start | bytes 2654212
  4.2 1.0 %copy-start.3 = (s32[98304]{0:T(1024)S(1)}, s32[98304]{0:T(1024)}, u32[]{:S(2)}) copy-start(s32[98304]{0:T(1024)} %param.10) | copy-start | bytes 1179652
  69.0 1.0 %copy-start = (bf16[2048,256]{1,0:T(8,128)(2,1)}, bf16[2048,256]{1,0:T(8,128)(2,1)S(1)}, u32[]{:S(2)}) copy-start(bf16[2048,256]{1,0:T(8,128)(2,1)S(1)} %get-tuple-element.7.spread_ref) | copy-start | bytes 3145732
  70.0 0.8 %copy-start.2 = (bf16[256,1152]{1,0:T(8,128)(2,1)}, bf16[256,1152]{1,0:T(8,128)(2,1)S(1)}, u32[]{:S(2)}) copy-start(bf16[256,1152]{1,0:T(8,128)(2,1)S(1)} %get-tuple-element.8.back_ref) | copy-start | bytes 1769476

commit v2 on v1

v2 whole, which is shorter than its diff:
```python
import jax
import jax.numpy as jnp
from jax import lax
from jax.experimental import pallas as pl
from jax.experimental.pallas import tpu as pltpu
from jax.sharding import PartitionSpec as P

MESH = pl.DeviceIdType.MESH
GRID = 16
NZ, NX, NY = 8, 4, 4
SLOT = 8
EPS = 1e-06
BF16, F32, I32 = jnp.bfloat16, jnp.float32, jnp.int32

ORDER = (4, 3, 5, 2, 6, 1, 7, 0)
PLACE = {rel: k for k, rel in enumerate(ORDER)}
NEAR = (0, 1, 7, 2, 6, 3, 5, 4)
ISSUE = NEAR
POOL_EARLY = 2
LATE_OWN = 1
LATE_PASS = 2
LATE_REST = 4
LANES = 128


def place():
    img, phr = lax.axis_index("img"), lax.axis_index("phr")
    return img // 4, (phr // 4) * 2 + (img // 2) % 2, phr % 4, img % 2


def device_at(z, x, y, c):
    z, x, y, c = lax.rem(z, NZ), lax.rem(x, NX), lax.rem(y, NY), lax.rem(c, 2)
    return ((z * 2 + lax.rem(x, 2)) * 2 + c, (x // 2) * 4 + y)


def iota(shape, dim):
    return lax.broadcasted_iota(I32, shape, dim)


def dot(a, b):
    return jnp.dot(a, b, preferred_element_type=F32)


def fold(value):
    groups, keep = value.shape[0] // SLOT, value.shape[1] - LANES
    value = value.reshape(groups, SLOT, keep + LANES)
    tiles = [value[:, t : t + 1, keep:] for t in range(SLOT - 1)]
    tiles.append(jnp.zeros((groups, 1, keep - (SLOT - 1) * LANES), F32))
    spare = iota((groups, SLOT, keep), 1) == SLOT - 1
    folded = jnp.where(spare, jnp.concatenate(tiles, axis=2), value[:, :, :keep])
    return folded.reshape(groups * SLOT, keep)


def folded_columns(folded):
    groups, keep = folded.shape[0] // SLOT, folded.shape[1]
    folded = folded.reshape(groups, SLOT, keep)
    row = iota((groups, SLOT, LANES), 1)
    columns = jnp.zeros((groups, SLOT, LANES), F32)
    for t in range(SLOT - 1):
        tile = folded[:, SLOT - 1 : SLOT, t * LANES : (t + 1) * LANES]
        columns = jnp.where(row == t, tile, columns)
    return columns.reshape(groups * SLOT, LANES)


def exchange_kernel(
    sharp_hbm,
    shift_hbm,
    limits_hbm,
    shard_hbm,
    named_hbm,
    phrase_hbm,
    feature_hbm,
    back_hbm,
    spread_hbm,
    feature,
    raw,
    named,
    sharp_ref,
    shift_ref,
    limits_ref,
    flat_ref,
    shard_ref,
    phrases,
    pool,
    z_out,
    z_in,
    x_out,
    x_in,
    regions,
    unit,
    ids,
    inverse,
    total,
    p_out,
    p_in,
    s_out,
    spread,
    in_sem,
    feature_sem,
    y_send,
    y_recv,
    zf_send,
    zf_recv,
    xf_send,
    xf_recv,
    xr_send,
    xr_recv,
    zr_send,
    zr_recv,
):
    z, x, y, c = place()
    me_img, me_phr = lax.axis_index("img"), lax.axis_index("phr")
    shard = me_img
    reg_dev = limits_ref.shape[1]
    n_dev = shard_ref.shape[0]
    ph_dev = raw.shape[0]
    half = ph_dev // 2
    reg_img = 12
    patches = GRID * GRID
    n_feature = feature_sem.shape[0]
    chunk = feature.shape[0] // n_feature

    def remote(src, dst, send, recv, dz=0, dx=0, dy=0, dc=0):
        return pltpu.make_async_remote_copy(
            src_ref=src,
            dst_ref=dst,
            send_sem=send,
            recv_sem=recv,
            device_id=device_at(z + dz % NZ, x + dx % NX, y + dy % NY, c + dc),
            device_id_type=MESH,
        )

    phrase_copy = pltpu.make_async_copy(phrase_hbm, raw, in_sem.at[0])
    phrase_copy.start()
    limits_copy = pltpu.make_async_copy(limits_hbm, limits_ref, in_sem.at[2])
    limits_copy.start()
    shard_copy = pltpu.make_async_copy(shard_hbm, flat_ref, in_sem.at[3])
    shard_copy.start()
    feature_copies = []
    for i in range(n_feature):
        rows = pl.ds(i * chunk, chunk)
        copy = pltpu.make_async_copy(feature_hbm.at[rows], feature.at[rows], feature_sem.at[i])
        copy.start()
        feature_copies.append(copy)
    sharp_copy = pltpu.make_async_copy(sharp_hbm, sharp_ref, in_sem.at[6])
    sharp_copy.start()
    shift_copy = pltpu.make_async_copy(shift_hbm, shift_ref, in_sem.at[7])
    shift_copy.start()
    named_copy = pltpu.make_async_copy(named_hbm.at[pl.ds(shard * 24, 24)], named, in_sem.at[1])
    named_copy.start()

    barrier = pltpu.get_barrier_semaphore()
    partners = [(dz, 0, 0, dc) for dz in range(NZ) for dc in range(2) if (dz, dc) != (0, 0)]
    partners += [(0, dx, 0, 0) for dx in range(1, NX)] + [(0, 0, 1, 0), (0, 0, 3, 0)]
    for dz, dx, dy, dc in partners:
        pl.semaphore_signal(
            barrier, inc=1, device_id=device_at(z + dz, x + dx, y + dy, c + dc), device_id_type=MESH
        )

    phrase_copy.wait()
    for i in range(0, ph_dev, 64):
        rows = pl.ds(i, 64)
        own = raw[rows].astype(F32)
        scale = lax.rsqrt(jnp.sum(own * own, axis=1, keepdims=True) + EPS)
        phrases[rows] = (own * scale).astype(BF16)
    shard_copy.wait()
    groups = n_dev // 4
    wide = jnp.concatenate([flat_ref[pl.ds(i, groups, stride=3), :] for i in range(3)], axis=1)
    for i in range(4):
        shard_ref[pl.ds(i * groups, groups)] = wide[:, i * reg_dev : (i + 1) * reg_dev]

    def shard_row(device):
        return (device & 3) * groups + (device >> 2)

    own = shard_ref[pl.ds(shard_row(me_img * 8 + me_phr), 1), :]
    member = (iota((32, reg_dev), 0) == own).astype(F32)
    earlier = (iota((reg_dev, reg_dev), 0) < iota((reg_dev, reg_dev), 1)).astype(BF16)
    rank = jnp.sum(member * dot(member.astype(BF16), earlier), axis=0, keepdims=True).astype(I32)
    parity = lax.rem(x, 2)
    to_z = ((own >> 2) - z + NZ) & (NZ - 1)
    to_c = jnp.where((own & 1) == c, 0, 1)
    to_x = jnp.where(((own >> 1) & 1) == parity, 0, 1)
    goes = ((to_z * 2 + to_c) * 2 + to_x) * SLOT + rank
    slots = NZ * 4 * SLOT
    dispatch = (iota((slots, reg_dev), 0) == goes).astype(BF16)

    limits_copy.wait()
    same = iota((reg_dev, reg_dev), 0) == iota((reg_dev, reg_dev), 1)

    def as_column(row):
        return jnp.sum(jnp.where(same, row.astype(F32), 0.0), axis=1, keepdims=True).astype(I32)

    limit = [limits_ref[j : j + 1, :] for j in range(4)]
    limit_column = [as_column(row) for row in limit]
    spot = iota((reg_dev, patches), 1)
    spot_row, spot_col = spot >> 4, spot & 15
    inside = (
        (spot_row >= limit_column[0])
        & (spot_row < limit_column[1])
        & (spot_col >= limit_column[2])
        & (spot_col < limit_column[3])
    )
    region = iota((reg_dev, patches), 0)
    images = chunk // patches

    def pool_chunk(i):
        feature_copies[i].wait()
        mask = jnp.concatenate(
            [
                (
                    inside
                    & (region >= (i * images + m) * reg_img)
                    & (region < (i * images + m + 1) * reg_img)
                ).astype(F32)
                for m in range(images)
            ],
            axis=1,
        ).astype(BF16)
        term = dot(mask, feature[pl.ds(i * chunk, chunk)])
        pool[...] = term if i == 0 else pool[...] + term

    for i in range(POOL_EARLY):
        pool_chunk(i)
    pl.semaphore_wait(barrier, len(partners))

    def ring(index, block, to_block, first, count, dy):
        return remote(
            phrases.at[pl.ds(block * ph_dev + first, count)],
            phrases.at[pl.ds(to_block * ph_dev + first, count)],
            y_send.at[index],
            y_recv.at[index],
            dy=dy,
        )

    ring_copies = [
        ring(0, 0, 1, 0, half, 1),
        ring(1, 0, 2, half, half, -1),
        ring(2, 0, 1, half, half, 1),
        ring(3, 0, 2, 0, half, -1),
        ring(4, 1, 3, 0, LANES, 1),
        ring(5, 2, 3, ph_dev - LANES, LANES, -1),
        ring(6, 1, 3, LANES, half - LANES, 1),
        ring(7, 2, 3, half, half - LANES, -1),
    ]
    for copy in ring_copies[: 2 if LATE_OWN else 4]:
        copy.start()

    for i in range(POOL_EARLY, n_feature):
        pool_chunk(i)
    z_out[...] = fold(dot(dispatch, pool[...].astype(BF16))).astype(BF16)

    def block(ref, index):
        return ref.at[pl.ds(index * 2 * SLOT, 2 * SLOT)]

    z_copies = {}
    for dz in ISSUE:
        for dc in range(2):
            if (dz, dc) == (0, 0):
                continue
            there = (NZ - dz) % NZ
            copy = remote(
                block(z_out, dz * 2 + dc),
                block(z_in, there * 2 + dc),
                zf_send.at[dz, dc],
                zf_recv.at[there, dc],
                dz=dz,
                dc=dc,
            )
            copy.start()
            z_copies[dz, dc] = copy

    live = 4 * NZ * 2 * SLOT
    member_all = (shard_ref[...] == shard).astype(BF16)
    rank_all = dot(member_all, earlier).astype(BF16)
    slot = iota((live, n_dev), 0)
    k, xr, dc_, r_ = slot >> 6, (slot >> 4) & 3, (slot >> 3) & 1, slot & 7
    rel = jnp.zeros_like(k)
    for rel_z, at in PLACE.items():
        rel = jnp.where(k == at, rel_z, rel)
    from_z = (z + rel) & (NZ - 1)
    from_x = (x + xr) & (NX - 1)
    from_c = (c + dc_) & 1
    device = ((from_z * 2 + (from_x & 1)) * 2 + from_c) * 8 + (from_x >> 1) * 4 + y
    pick = (iota((live, n_dev), 1) == shard_row(device)).astype(BF16)
    member_slot = dot(pick, member_all)
    rank_slot = dot(pick, rank_all)
    wanted = r_[:, :reg_dev].astype(F32)
    local = (iota((live, reg_dev), 1) + 1).astype(F32)
    held = jnp.sum(
        jnp.where(rank_slot == wanted, member_slot * local, 0.0), axis=1, keepdims=True
    ).astype(I32)
    ids[...] = jnp.where(held > 0, device[:, :128] * reg_dev + held - 1, -1)

    collect = (iota((reg_dev, slots), 1) == as_column(goes)).astype(BF16)
    spot = iota((patches, reg_dev), 0)
    spot_row, spot_col = spot >> 4, spot & 15
    inside = (
        (spot_row >= limit[0])
        & (spot_row < limit[1])
        & (spot_col >= limit[2])
        & (spot_col < limit[3])
    )
    region = iota((patches, reg_dev), 1)
    for m in range(reg_dev // reg_img):
        mask = (inside & (region >= m * reg_img) & (region < (m + 1) * reg_img)).astype(BF16)
        spread[pl.ds(m * patches, patches)] = dot(mask, collect).astype(BF16)
    spread_copy = pltpu.make_async_copy(spread, spread_hbm, in_sem.at[4])
    spread_copy.start()

    x_copies = {}
    for step, rel in enumerate(NEAR):
        at = PLACE[rel]
        if LATE_OWN and step == LATE_OWN:
            ring_copies[2].start()
            ring_copies[3].start()
        if step == LATE_PASS:
            ring_copies[0].wait_recv()
            ring_copies[4].start()
            ring_copies[1].wait_recv()
            ring_copies[5].start()
        if step == LATE_REST:
            ring_copies[6].start()
            ring_copies[7].start()
        sides = []
        for dc in range(2):
            if (rel, dc) == (0, 0):
                got = block(z_out, 0)
            else:
                got = block(z_in, rel * 2 + dc)
                z_copies[(NZ - rel) % NZ, dc].wait_recv()
            sides.append(got[...].astype(F32))
        near, far = [
            jnp.concatenate(
                [side[p * SLOT : (p + 1) * SLOT] for side in sides], axis=0
            ).astype(BF16)
            for p in range(2)
        ]
        block(x_in, at * 4)[...] = near
        block(x_out, rel * 2)[...] = near
        block(x_out, rel * 2 + 1)[...] = far
        for dx in (2, 1, 3):
            there = NX - dx
            copy = remote(
                block(x_out, rel * 2 + dx % 2),
                block(x_in, at * 4 + there),
                xf_send.at[rel, dx - 1],
                xf_recv.at[rel, there - 1],
                dx=dx,
            )
            copy.start()
            x_copies[rel, dx] = copy

    named_copy.wait()
    sharp_copy.wait()
    shift_copy.wait()
    sharp, shift = sharp_ref[0], shift_ref[0]
    for rel in NEAR:
        for dx in (2, 1, 3):
            x_copies[rel, dx].wait_recv()
        rows = pl.ds(PLACE[rel] * 64, 64)
        folded = x_in[rows].astype(F32)
        arrived = jnp.concatenate([folded, folded_columns(folded)], axis=1)
        inv = lax.rsqrt(jnp.sum(arrived * arrived, axis=1, keepdims=True) + EPS)
        regions[rows] = arrived.astype(BF16)
        inverse[rows] = jnp.broadcast_to(inv, (64, LANES))
        unit[rows] = (arrived * inv).astype(BF16)

    def pairs(rows, which, first, count, dy):
        them = phrases[pl.ds(which * ph_dev + first, count)]
        scores = lax.dot_general(
            unit[rows], them, (((1,), (1,)), ((), ())), preferred_element_type=F32
        )
        row = (me_phr // 4) * 12 + lax.rem(y + dy, NY) * 3 + first // LANES
        mine = ids[rows]
        weights = []
        for j in range(count // LANES):
            logits = sharp * scores[:, j * LANES : (j + 1) * LANES] + shift
            positive = (mine == named[pl.ds(row + j, 1), :]).astype(F32)
            weights.append((jax.nn.sigmoid(logits) - positive).astype(BF16))
        return dot(jnp.concatenate(weights, axis=1), them)

    everything = pl.ds(0, live)
    total[...] = pairs(everything, 0, 0, ph_dev, 0)
    ring_copies[2].wait_recv()
    total[...] += pairs(everything, 1, 0, ph_dev, 3)
    ring_copies[3].wait_recv()
    total[...] += pairs(everything, 2, 0, ph_dev, 1)
    ring_copies[4].wait_recv()
    total[...] += pairs(everything, 3, 0, LANES, 2)
    ring_copies[5].wait_recv()
    total[...] += pairs(everything, 3, ph_dev - LANES, LANES, 2)
    ring_copies[6].wait_recv()
    ring_copies[7].wait_recv()
    r_copies = {}
    for part in range(2):
        rows = pl.ds(part * (live // 2), live // 2)
        total[rows] += pairs(rows, 3, LANES, LANES, 2)
        for at in range(part * 4, part * 4 + 4):
            rows = pl.ds(at * 64, 64)
            pull = sharp * total[rows]
            arrived = regions[rows].astype(F32)
            inv = inverse[rows][:, 0:1]
            radial = jnp.sum(arrived * pull, axis=1, keepdims=True)
            p_out[rows] = fold(inv * pull - (inv * inv * inv * radial) * arrived).astype(BF16)
            for dx in (2, 1, 3):
                there = NX - dx
                copy = remote(
                    block(p_out, at * 4 + dx),
                    block(p_in, at * 4 + there),
                    xr_send.at[at, dx - 1],
                    xr_recv.at[at, there - 1],
                    dx=dx,
                )
                copy.start()
                r_copies[at, dx] = copy

    home_copies = {}
    for at, rel in enumerate(ORDER):
        for dx in (2, 1, 3):
            r_copies[at, dx].wait_recv()
        near = block(p_out, at * 4)[...].astype(F32) + block(p_in, at * 4 + 2)[...].astype(F32)
        far = block(p_in, at * 4 + 1)[...].astype(F32) + block(p_in, at * 4 + 3)[...].astype(F32)
        there = (NZ - rel) % NZ
        for dc in range(2):
            rows = slice(dc * SLOT, (dc + 1) * SLOT)
            block(s_out, at * 2 + dc)[...] = jnp.concatenate(
                [near[rows], far[rows]], axis=0
            ).astype(BF16)
            if (rel, dc) == (0, 0):
                stay = pltpu.make_async_copy(block(s_out, at * 2), block(back_hbm, 0), in_sem.at[5])
                stay.start()
                continue
            copy = remote(
                block(s_out, at * 2 + dc),
                block(back_hbm, there * 2 + dc),
                zr_send.at[rel, dc],
                zr_recv.at[there, dc],
                dz=rel,
                dc=dc,
            )
            copy.start()
            home_copies[rel, dc] = copy

    for copy in home_copies.values():
        copy.wait_recv()
    stay.wait()
    spread_copy.wait()
    for copies in (ring_copies, z_copies.values(), x_copies.values(), r_copies.values(), home_copies.values()):
        for copy in copies:
            copy.wait_send()


def spread_kernel(spread_hbm, back_hbm, out_hbm, spread, back, last, staged, in_sems, out_sems):
    keep = back.shape[1]
    n_chunk = out_sems.shape[0]
    rows = spread.shape[0] // n_chunk
    loads, stores = [], []
    back_copy = pltpu.make_async_copy(back_hbm, back, in_sems.at[n_chunk])
    back_copy.start()
    for i in range(n_chunk):
        part = pl.ds(i * rows, rows)
        loads.append(pltpu.make_async_copy(spread_hbm.at[part], spread.at[part], in_sems.at[i]))
        loads[i].start()
    back_copy.wait()
    last[...] = folded_columns(back[...].astype(F32)).astype(BF16)
    for i in range(n_chunk):
        part = pl.ds(i * rows, rows)
        loads[i].wait()
        staged[part, pl.ds(0, keep)] = dot(spread[part], back[...]).astype(BF16)
        staged[part, pl.ds(keep, LANES)] = dot(spread[part], last[...]).astype(BF16)
        stores.append(pltpu.make_async_copy(staged.at[part], out_hbm.at[part], out_sems.at[i]))
        stores[i].start()
    for copy in stores:
        copy.wait()


def shards(features, limits, shard_index, named, phrases, sharpness, shift):
    images, patches, width = features.shape
    reg_dev, ph_dev = limits.shape[0], phrases.shape[0]
    n_dev = shard_index.shape[0] // reg_dev
    slots = NZ * 4 * SLOT
    live = slots * 2
    keep = width - LANES
    hbm = pl.BlockSpec(memory_space=pltpu.HBM)
    dma = pltpu.SemaphoreType.DMA
    back, spread = pl.pallas_call(
        exchange_kernel,
        out_shape=(
            jax.ShapeDtypeStruct((slots, keep), BF16),
            jax.ShapeDtypeStruct((images * patches, slots), BF16),
        ),
        in_specs=[hbm] * 7,
        out_specs=(hbm, hbm),
        scratch_shapes=[
            pltpu.VMEM((images * patches, width), BF16),
            pltpu.VMEM((ph_dev, width), BF16),
            pltpu.VMEM((24, LANES), I32),
            pltpu.SMEM((1,), F32),
            pltpu.SMEM((1,), F32),
            pltpu.VMEM((4, reg_dev), I32),
            pltpu.VMEM((n_dev * reg_dev // LANES, LANES), I32),
            pltpu.VMEM((n_dev, reg_dev), I32),
            pltpu.VMEM((NY * ph_dev, width), BF16),
            pltpu.VMEM((reg_dev, width), F32),
            pltpu.VMEM((slots, keep), BF16),
            pltpu.VMEM((slots, keep), BF16),
            pltpu.VMEM((slots, keep), BF16),
            pltpu.VMEM((live, keep), BF16),
            pltpu.VMEM((live, width), BF16),
            pltpu.VMEM((live, width), BF16),
            pltpu.VMEM((live, LANES), I32),
            pltpu.VMEM((live, LANES), F32),
            pltpu.VMEM((live, width), F32),
            pltpu.VMEM((live, keep), BF16),
            pltpu.VMEM((live, keep), BF16),
            pltpu.VMEM((slots, keep), BF16),
            pltpu.VMEM((images * patches, slots), BF16),
            dma((8,)),
            dma((4,)),
            dma((8,)),
            dma((8,)),
            dma((NZ, 2)),
            dma((NZ, 2)),
            dma((NZ, 3)),
            dma((NZ, 3)),
            dma((NZ, 3)),
            dma((NZ, 3)),
            dma((NZ, 2)),
            dma((NZ, 2)),
        ],
        compiler_params=pltpu.CompilerParams(
            collective_id=0, has_side_effects=True, vmem_limit_bytes=62 * 2**20
        ),
    )(
        sharpness,
        shift,
        limits.T,
        shard_index.reshape(-1, 128),
        named.reshape(-1, 128),
        phrases,
        features.reshape(images * patches, width),
    )
    out = pl.pallas_call(
        spread_kernel,
        out_shape=jax.ShapeDtypeStruct((images * patches, width), BF16),
        in_specs=[hbm, hbm],
        out_specs=hbm,
        scratch_shapes=[
            pltpu.VMEM((images * patches, slots), BF16),
            pltpu.VMEM((slots, keep), BF16),
            pltpu.VMEM((slots, LANES), BF16),
            pltpu.VMEM((images * patches, width), BF16),
            dma((9,)),
            dma((8,)),
        ],
        compiler_params=pltpu.CompilerParams(vmem_limit_bytes=62 * 2**20),
    )(spread, back)
    return out.reshape(images, patches, width)


def solution(mesh):
    return jax.shard_map(
        shards,
        mesh=mesh,
        in_specs=(
            P(("img", "phr"), None, None),
            P(("img", "phr"), None),
            P(),
            P(),
            P(("img", "phr"), None),
            P(),
            P(),
        ),
        out_specs=P(("img", "phr"), None, None),
        check_vma=False,
    )
```

time: 78.5 us -> 68.4 us (0.87)
  local copies, waits for them, and re-layouts: 5.7 us -> 0 us
  Pallas kernels: 71.1 us -> 66.9 us
    unnamed x9 -> x0, local copies, waits for them, and re-layouts: 4.72 us -> none
    pallas_call x2, Pallas kernels: 71.1 us -> 66.9 us  [the longest x1 61.8 us: shards(): pl.pallas_call(exchange_kernel, out_shape=(jax.ShapeDtypeStruct((slots, k...]
    reshape x1 -> x0, local copies, waits for them, and re-layouts: 0.98 us -> none  [shards(): shard_index.reshape(-1, reg_dev)]
where the time goes in v2:
time: 68.4 us; the launch traced here: 68.2 us
  Pallas kernels  66.9 us (98%)
  between operations  1.3 us (2%)
    pallas_call x1, Pallas kernels, shards(): pl.pallas_call(exchange_kernel, out_shape=(jax.ShapeDtypeStruct((slots, k...  61.8 us
    pallas_call x1, Pallas kernels, shards(): pl.pallas_call(spread_kernel, out_shape=jax.ShapeDtypeStruct((images * pa...  5.14 us

profile of v2, /device:TPU:1, one launch (start us, length us, event | category | flops | bytes accessed | tf_op | source)
XLA Modules:
  0.0 68.2 jit_solution(9982025827236423381)
XLA Ops:
  1.3 61.8 %shard_map.73 = (bf16[256,1024]{1,0:T(8,128)(2,1)}, bf16[2048,256]{1,0:T(8,128)(2,1)}) custom-call(f32[1]{0:T(128)S(6)} %copy.8.sharp_hbm, f32[1]{0:T(128)S(6)} %copy.9.shift_hbm, s32[4,96]{1,0:T(4,128)} %bitcast.8, s32[192,128]{1,0:T(8,128)} %bitcast.7, s32[768,128]{1,0:T(8,128)} %bitcast.6, bf16[384,1152]{1,0:T(8,128)(2,1)} %phrase_hbm.1, ...), custom_call_target="tpu_custom_call" | custom-call | tf_op jit(solution)/shard_map/pallas_call | solution.py:486
  63.1 5.1 %shard_map.74 = bf16[2048,1152]{1,0:T(8,128)(2,1)} custom-call(bf16[2048,256]{1,0:T(8,128)(2,1)} %get-tuple-element.7.spread_hbm, bf16[256,1024]{1,0:T(8,128)(2,1)} %get-tuple-element.8.back_hbm), custom_call_target="tpu_custom_call" | custom-call | tf_op jit(solution)/shard_map/pallas_call | solution.py:543

commit v3 on v2

--- a/solution.py
+++ b/solution.py
@@ -14,12 +14,12 @@
 
 ORDER = (4, 3, 5, 2, 6, 1, 7, 0)
 PLACE = {rel: k for k, rel in enumerate(ORDER)}
-NEAR = (0, 1, 7, 2, 6, 3, 5, 4)
+NEAR = (0, 1, 7, 6, 2, 5, 3, 4)
 ISSUE = NEAR
-POOL_EARLY = 2
+PARTS = ((0, 2), (2, 4), (4, 8))
 LATE_OWN = 1
-LATE_PASS = 2
-LATE_REST = 4
+LATE_PASS = 5
+LATE_REST = 7
 LANES = 128
 
 
@@ -80,6 +80,7 @@
     limits_ref,
     flat_ref,
     shard_ref,
+    ring_in,
     phrases,
     pool,
     z_out,
@@ -107,6 +108,7 @@
     xr_recv,
     zr_send,
     zr_recv,
+    ready,
 ):
     z, x, y, c = place()
     me_img, me_phr = lax.axis_index("img"), lax.axis_index("phr")
@@ -130,8 +132,6 @@
             device_id_type=MESH,
         )
 
-    phrase_copy = pltpu.make_async_copy(phrase_hbm, raw, in_sem.at[0])
-    phrase_copy.start()
     limits_copy = pltpu.make_async_copy(limits_hbm, limits_ref, in_sem.at[2])
     limits_copy.start()
     shard_copy = pltpu.make_async_copy(shard_hbm, flat_ref, in_sem.at[3])
@@ -146,23 +146,58 @@
     sharp_copy.start()
     shift_copy = pltpu.make_async_copy(shift_hbm, shift_ref, in_sem.at[7])
     shift_copy.start()
+    phrase_copy = pltpu.make_async_copy(phrase_hbm, raw, in_sem.at[0])
+    phrase_copy.start()
     named_copy = pltpu.make_async_copy(named_hbm.at[pl.ds(shard * 24, 24)], named, in_sem.at[1])
     named_copy.start()
 
+    def tell(semaphore, partners):
+        for dz, dx, dy, dc in partners:
+            pl.semaphore_signal(
+                semaphore,
+                inc=1,
+                device_id=device_at(z + dz, x + dx, y + dy, c + dc),
+                device_id_type=MESH,
+            )
+
     barrier = pltpu.get_barrier_semaphore()
-    partners = [(dz, 0, 0, dc) for dz in range(NZ) for dc in range(2) if (dz, dc) != (0, 0)]
-    partners += [(0, dx, 0, 0) for dx in range(1, NX)] + [(0, 0, 1, 0), (0, 0, 3, 0)]
-    for dz, dx, dy, dc in partners:
-        pl.semaphore_signal(
-            barrier, inc=1, device_id=device_at(z + dz, x + dx, y + dy, c + dc), device_id_type=MESH
+    along_x, along_y = [(0, 1, 0, 0), (0, 3, 0, 0)], [(0, 0, 1, 0), (0, 0, 3, 0)]
+    along_z = [(1, 0, 0, 0), (7, 0, 0, 0)]
+    neighbours = along_y + [(0, 0, 0, 1)] + along_x + along_z
+    tell(barrier, neighbours)
+    pl.semaphore_wait(barrier, len(neighbours))
+
+    def ring(index, block, to_block, first, count, dy):
+        source = phrase_hbm if block == 0 else ring_in
+        return remote(
+            source.at[pl.ds(max(block - 1, 0) * ph_dev + first, count)],
+            ring_in.at[pl.ds((to_block - 1) * ph_dev + first, count)],
+            y_send.at[index],
+            y_recv.at[index],
+            dy=dy,
         )
 
-    phrase_copy.wait()
-    for i in range(0, ph_dev, 64):
-        rows = pl.ds(i, 64)
-        own = raw[rows].astype(F32)
-        scale = lax.rsqrt(jnp.sum(own * own, axis=1, keepdims=True) + EPS)
-        phrases[rows] = (own * scale).astype(BF16)
+    ring_copies = [
+        ring(0, 0, 1, 0, half, 1),
+        ring(1, 0, 2, half, half, -1),
+        ring(2, 0, 1, half, half, 1),
+        ring(3, 0, 2, 0, half, -1),
+        ring(4, 1, 3, 0, LANES, 1),
+        ring(5, 2, 3, ph_dev - LANES, LANES, -1),
+        ring(6, 1, 3, LANES, half - LANES, 1),
+        ring(7, 2, 3, half, half - LANES, -1),
+    ]
+    for copy in ring_copies[: 2 if LATE_OWN else 4]:
+        copy.start()
+
+    tell(ready.at[0], along_x)
+    tell(ready.at[1], along_z)
+
+    def hear(step):
+        pl.semaphore_wait(ready.at[step], 2)
+        if step < 4:
+            tell(ready.at[step + 1], along_z)
+
     shard_copy.wait()
     groups = n_dev // 4
     wide = jnp.concatenate([flat_ref[pl.ds(i, groups, stride=3), :] for i in range(3)], axis=1)
@@ -219,34 +254,10 @@
         term = dot(mask, feature[pl.ds(i * chunk, chunk)])
         pool[...] = term if i == 0 else pool[...] + term
 
-    for i in range(POOL_EARLY):
+    for i in range(n_feature):
         pool_chunk(i)
-    pl.semaphore_wait(barrier, len(partners))
-
-    def ring(index, block, to_block, first, count, dy):
-        return remote(
-            phrases.at[pl.ds(block * ph_dev + first, count)],
-            phrases.at[pl.ds(to_block * ph_dev + first, count)],
-            y_send.at[index],
-            y_recv.at[index],
-            dy=dy,
-        )
-
-    ring_copies = [
-        ring(0, 0, 1, 0, half, 1),
-        ring(1, 0, 2, half, half, -1),
-        ring(2, 0, 1, half, half, 1),
-        ring(3, 0, 2, 0, half, -1),
-        ring(4, 1, 3, 0, LANES, 1),
-        ring(5, 2, 3, ph_dev - LANES, LANES, -1),
-        ring(6, 1, 3, LANES, half - LANES, 1),
-        ring(7, 2, 3, half, half - LANES, -1),
-    ]
-    for copy in ring_copies[: 2 if LATE_OWN else 4]:
-        copy.start()
-
-    for i in range(POOL_EARLY, n_feature):
-        pool_chunk(i)
+        hear(i + 1)
+    pl.semaphore_wait(ready.at[0], 2)
     z_out[...] = fold(dot(dispatch, pool[...].astype(BF16))).astype(BF16)
 
     def block(ref, index):
@@ -268,6 +279,16 @@
             )
             copy.start()
             z_copies[dz, dc] = copy
+
+    def to_unit(source, block, first, count):
+        for i in range(first, first + count, 64):
+            rows = pl.ds(max(block - 1, 0) * ph_dev + i, 64)
+            them = source[rows].astype(F32)
+            scale = lax.rsqrt(jnp.sum(them * them, axis=1, keepdims=True) + EPS)
+            phrases[pl.ds(block * ph_dev + i, 64)] = (them * scale).astype(BF16)
+
+    phrase_copy.wait()
+    to_unit(raw, 0, 0, ph_dev)
 
     live = 4 * NZ * 2 * SLOT
     member_all = (shard_ref[...] == shard).astype(BF16)
@@ -354,7 +375,8 @@
     sharp_copy.wait()
     shift_copy.wait()
     sharp, shift = sharp_ref[0], shift_ref[0]
-    for rel in NEAR:
+
+    def arrive(rel):
         for dx in (2, 1, 3):
             x_copies[rel, dx].wait_recv()
         rows = pl.ds(PLACE[rel] * 64, 64)
@@ -365,37 +387,45 @@
         inverse[rows] = jnp.broadcast_to(inv, (64, LANES))
         unit[rows] = (arrived * inv).astype(BF16)
 
-    def pairs(rows, which, first, count, dy):
-        them = phrases[pl.ds(which * ph_dev + first, count)]
+    def pairs(rows, first, count):
+        them = phrases[pl.ds(first, count)]
         scores = lax.dot_general(
             unit[rows], them, (((1,), (1,)), ((), ())), preferred_element_type=F32
         )
-        row = (me_phr // 4) * 12 + lax.rem(y + dy, NY) * 3 + first // LANES
         mine = ids[rows]
         weights = []
         for j in range(count // LANES):
+            block, inner = divmod(first + j * LANES, ph_dev)
+            row = (me_phr // 4) * 12 + lax.rem(y + (0, 3, 1, 2)[block], NY) * 3 + inner // LANES
             logits = sharp * scores[:, j * LANES : (j + 1) * LANES] + shift
-            positive = (mine == named[pl.ds(row + j, 1), :]).astype(F32)
+            positive = (mine == named[pl.ds(row, 1), :]).astype(F32)
             weights.append((jax.nn.sigmoid(logits) - positive).astype(BF16))
         return dot(jnp.concatenate(weights, axis=1), them)
 
-    everything = pl.ds(0, live)
-    total[...] = pairs(everything, 0, 0, ph_dev, 0)
+    everything, far_half, near_half = pl.ds(0, live), pl.ds(0, live // 2), pl.ds(live // 2, live // 2)
+    for rel in NEAR[:4]:
+        arrive(rel)
     ring_copies[2].wait_recv()
-    total[...] += pairs(everything, 1, 0, ph_dev, 3)
+    to_unit(ring_in, 1, 0, ph_dev)
+    total[near_half] = pairs(near_half, 0, 2 * ph_dev)
+    for rel in NEAR[4:]:
+        arrive(rel)
+    total[far_half] = pairs(far_half, 0, 2 * ph_dev)
     ring_copies[3].wait_recv()
-    total[...] += pairs(everything, 2, 0, ph_dev, 1)
+    to_unit(ring_in, 2, 0, ph_dev)
     ring_copies[4].wait_recv()
-    total[...] += pairs(everything, 3, 0, LANES, 2)
+    to_unit(ring_in, 3, 0, LANES)
+    total[...] += pairs(everything, 2 * ph_dev, ph_dev + LANES)
     ring_copies[5].wait_recv()
-    total[...] += pairs(everything, 3, ph_dev - LANES, LANES, 2)
+    to_unit(ring_in, 3, 2 * LANES, LANES)
     ring_copies[6].wait_recv()
     ring_copies[7].wait_recv()
+    to_unit(ring_in, 3, LANES, LANES)
     r_copies = {}
-    for part in range(2):
-        rows = pl.ds(part * (live // 2), live // 2)
-        total[rows] += pairs(rows, 3, LANES, LANES, 2)
-        for at in range(part * 4, part * 4 + 4):
+    for begin, end in PARTS:
+        rows = pl.ds(begin * 64, (end - begin) * 64)
+        total[rows] += pairs(rows, 3 * ph_dev + LANES, 2 * LANES)
+        for at in range(begin, end):
             rows = pl.ds(at * 64, 64)
             pull = sharp * total[rows]
             arrived = regions[rows].astype(F32)
@@ -452,24 +482,29 @@
 
 def spread_kernel(spread_hbm, back_hbm, out_hbm, spread, back, last, staged, in_sems, out_sems):
     keep = back.shape[1]
-    n_chunk = out_sems.shape[0]
-    rows = spread.shape[0] // n_chunk
+    half = spread.shape[0] // 2
+    back_copy = pltpu.make_async_copy(back_hbm, back, in_sems.at[2])
+    back_copy.start()
     loads, stores = [], []
-    back_copy = pltpu.make_async_copy(back_hbm, back, in_sems.at[n_chunk])
-    back_copy.start()
-    for i in range(n_chunk):
-        part = pl.ds(i * rows, rows)
+    for i in range(2):
+        part = pl.ds(i * half, half)
         loads.append(pltpu.make_async_copy(spread_hbm.at[part], spread.at[part], in_sems.at[i]))
         loads[i].start()
     back_copy.wait()
     last[...] = folded_columns(back[...].astype(F32)).astype(BF16)
-    for i in range(n_chunk):
-        part = pl.ds(i * rows, rows)
-        loads[i].wait()
-        staged[part, pl.ds(0, keep)] = dot(spread[part], back[...]).astype(BF16)
-        staged[part, pl.ds(keep, LANES)] = dot(spread[part], last[...]).astype(BF16)
-        stores.append(pltpu.make_async_copy(staged.at[part], out_hbm.at[part], out_sems.at[i]))
-        stores[i].start()
+    for first in range(0, keep + LANES, 2 * LANES):
+        columns = pl.ds(first, min(2 * LANES, keep + LANES - first))
+        slots = back[:, columns] if first < keep else last[...]
+        for i in range(2):
+            if first == 0:
+                loads[i].wait()
+            part = pl.ds(i * half, half)
+            staged[part, columns] = dot(spread[part], slots).astype(BF16)
+        copy = pltpu.make_async_copy(
+            staged.at[:, columns], out_hbm.at[:, columns], out_sems.at[len(stores)]
+        )
+        copy.start()
+        stores.append(copy)
     for copy in stores:
         copy.wait()
 
@@ -500,6 +535,7 @@
             pltpu.VMEM((4, reg_dev), I32),
             pltpu.VMEM((n_dev * reg_dev // LANES, LANES), I32),
             pltpu.VMEM((n_dev, reg_dev), I32),
+            pltpu.VMEM(((NY - 1) * ph_dev, width), BF16),
             pltpu.VMEM((NY * ph_dev, width), BF16),
             pltpu.VMEM((reg_dev, width), F32),
             pltpu.VMEM((slots, keep), BF16),
@@ -527,6 +563,7 @@
             dma((NZ, 3)),
             dma((NZ, 2)),
             dma((NZ, 2)),
+            pltpu.SemaphoreType.REGULAR((5,)),
         ],
         compiler_params=pltpu.CompilerParams(
             collective_id=0, has_side_effects=True, vmem_limit_bytes=62 * 2**20
@@ -550,8 +587,8 @@
             pltpu.VMEM((slots, keep), BF16),
             pltpu.VMEM((slots, LANES), BF16),
             pltpu.VMEM((images * patches, width), BF16),
-            dma((9,)),
-            dma((8,)),
+            dma((3,)),
+            dma((width // LANES // 2 + 1,)),
         ],
         compiler_params=pltpu.CompilerParams(vmem_limit_bytes=62 * 2**20),
     )(spread, back)

time: 68.4 us -> 65.6 us (0.959)
  Pallas kernels: 66.9 us -> 64.2 us
    pallas_call x1, Pallas kernels: 61.8 us -> 59.9 us  [shards(): pl.pallas_call(exchange_kernel, out_shape=(jax.ShapeDtypeStruct((slots, k...]
    pallas_call x1, Pallas kernels: 5.14 us -> 4.29 us  [shards(): pl.pallas_call(spread_kernel, out_shape=jax.ShapeDtypeStruct((images * pa...]
where the time goes in v3:
time: 65.6 us; the launch traced here: 65.5 us
  Pallas kernels  64.2 us (98%)
  between operations  1.3 us (2%)
    pallas_call x1, Pallas kernels, shards(): pl.pallas_call(exchange_kernel, out_shape=(jax.ShapeDtypeStruct((slots, k...  59.9 us
    pallas_call x1, Pallas kernels, shards(): pl.pallas_call(spread_kernel, out_shape=jax.ShapeDtypeStruct((images * pa...  4.29 us

profile of v3, /device:TPU:1, one launch (start us, length us, event | category | flops | bytes accessed | tf_op | source)
XLA Modules:
  0.0 65.5 jit_solution(11886467930851646686)
XLA Ops:
  1.3 59.9 %shard_map.73 = (bf16[256,1024]{1,0:T(8,128)(2,1)}, bf16[2048,256]{1,0:T(8,128)(2,1)}) custom-call(f32[1]{0:T(128)S(6)} %copy.8.sharp_hbm, f32[1]{0:T(128)S(6)} %copy.9.shift_hbm, s32[4,96]{1,0:T(4,128)} %bitcast.8, s32[192,128]{1,0:T(8,128)} %bitcast.7, s32[768,128]{1,0:T(8,128)} %bitcast.6, bf16[384,1152]{1,0:T(8,128)(2,1)} %phrase_hbm.1, ...), custom_call_target="tpu_custom_call" | custom-call | tf_op jit(solution)/shard_map/pallas_call | solution.py:521
  61.2 4.3 %shard_map.74 = bf16[2048,1152]{1,0:T(8,128)(2,1)} custom-call(bf16[2048,256]{1,0:T(8,128)(2,1)} %get-tuple-element.7.spread_hbm, bf16[256,1024]{1,0:T(8,128)(2,1)} %get-tuple-element.8.back_hbm), custom_call_target="tpu_custom_call" | custom-call | tf_op jit(solution)/shard_map/pallas_call | solution.py:580

commit v4 on v3

--- a/solution.py
+++ b/solution.py
@@ -16,10 +16,10 @@
 PLACE = {rel: k for k, rel in enumerate(ORDER)}
 NEAR = (0, 1, 7, 6, 2, 5, 3, 4)
 ISSUE = NEAR
-PARTS = ((0, 2), (2, 4), (4, 8))
+PARTS = ((0, 4), (4, 8))
+LEAD = 4
 LATE_OWN = 1
-LATE_PASS = 5
-LATE_REST = 7
+LATE_PASS = 3
 LANES = 128
 
 
@@ -187,7 +187,7 @@
         ring(6, 1, 3, LANES, half - LANES, 1),
         ring(7, 2, 3, half, half - LANES, -1),
     ]
-    for copy in ring_copies[: 2 if LATE_OWN else 4]:
+    for copy in ring_copies[:2]:
         copy.start()
 
     tell(ready.at[0], along_x)
@@ -331,7 +331,7 @@
     x_copies = {}
     for step, rel in enumerate(NEAR):
         at = PLACE[rel]
-        if LATE_OWN and step == LATE_OWN:
+        if step == LATE_OWN:
             ring_copies[2].start()
             ring_copies[3].start()
         if step == LATE_PASS:
@@ -339,9 +339,6 @@
             ring_copies[4].start()
             ring_copies[1].wait_recv()
             ring_copies[5].start()
-        if step == LATE_REST:
-            ring_copies[6].start()
-            ring_copies[7].start()
         sides = []
         for dc in range(2):
             if (rel, dc) == (0, 0):
@@ -405,6 +402,8 @@
     everything, far_half, near_half = pl.ds(0, live), pl.ds(0, live // 2), pl.ds(live // 2, live // 2)
     for rel in NEAR[:4]:
         arrive(rel)
+    ring_copies[6].start()
+    ring_copies[7].start()
     ring_copies[2].wait_recv()
     to_unit(ring_in, 1, 0, ph_dev)
     total[near_half] = pairs(near_half, 0, 2 * ph_dev)
@@ -422,29 +421,33 @@
     ring_copies[7].wait_recv()
     to_unit(ring_in, 3, LANES, LANES)
     r_copies = {}
-    for begin, end in PARTS:
-        rows = pl.ds(begin * 64, (end - begin) * 64)
-        total[rows] += pairs(rows, 3 * ph_dev + LANES, 2 * LANES)
-        for at in range(begin, end):
-            rows = pl.ds(at * 64, 64)
-            pull = sharp * total[rows]
-            arrived = regions[rows].astype(F32)
-            inv = inverse[rows][:, 0:1]
-            radial = jnp.sum(arrived * pull, axis=1, keepdims=True)
-            p_out[rows] = fold(inv * pull - (inv * inv * inv * radial) * arrived).astype(BF16)
-            for dx in (2, 1, 3):
-                there = NX - dx
-                copy = remote(
-                    block(p_out, at * 4 + dx),
-                    block(p_in, at * 4 + there),
-                    xr_send.at[at, dx - 1],
-                    xr_recv.at[at, there - 1],
-                    dx=dx,
-                )
-                copy.start()
-                r_copies[at, dx] = copy
+
+    def give(at):
+        for begin, end in PARTS:
+            if at == begin:
+                rows = pl.ds(begin * 64, (end - begin) * 64)
+                total[rows] += pairs(rows, 3 * ph_dev + LANES, 2 * LANES)
+        rows = pl.ds(at * 64, 64)
+        pull = sharp * total[rows]
+        arrived = regions[rows].astype(F32)
+        inv = inverse[rows][:, 0:1]
+        radial = jnp.sum(arrived * pull, axis=1, keepdims=True)
+        p_out[rows] = fold(inv * pull - (inv * inv * inv * radial) * arrived).astype(BF16)
+        for dx in (2, 1, 3):
+            there = NX - dx
+            copy = remote(
+                block(p_out, at * 4 + dx),
+                block(p_in, at * 4 + there),
+                xr_send.at[at, dx - 1],
+                xr_recv.at[at, there - 1],
+                dx=dx,
+            )
+            copy.start()
+            r_copies[at, dx] = copy
 
     home_copies = {}
+    for at in range(LEAD):
+        give(at)
     for at, rel in enumerate(ORDER):
         for dx in (2, 1, 3):
             r_copies[at, dx].wait_recv()
@@ -470,6 +473,8 @@
             )
             copy.start()
             home_copies[rel, dc] = copy
+        if at + LEAD < NZ:
+            give(at + LEAD)
 
     for copy in home_copies.values():
         copy.wait_recv()
@@ -491,20 +496,21 @@
         loads.append(pltpu.make_async_copy(spread_hbm.at[part], spread.at[part], in_sems.at[i]))
         loads[i].start()
     back_copy.wait()
-    last[...] = folded_columns(back[...].astype(F32)).astype(BF16)
     for first in range(0, keep + LANES, 2 * LANES):
         columns = pl.ds(first, min(2 * LANES, keep + LANES - first))
+        if first == keep:
+            last[...] = folded_columns(back[...].astype(F32)).astype(BF16)
         slots = back[:, columns] if first < keep else last[...]
         for i in range(2):
             if first == 0:
                 loads[i].wait()
             part = pl.ds(i * half, half)
             staged[part, columns] = dot(spread[part], slots).astype(BF16)
-        copy = pltpu.make_async_copy(
-            staged.at[:, columns], out_hbm.at[:, columns], out_sems.at[len(stores)]
-        )
-        copy.start()
-        stores.append(copy)
+            copy = pltpu.make_async_copy(
+                staged.at[part, columns], out_hbm.at[part, columns], out_sems.at[len(stores)]
+            )
+            copy.start()
+            stores.append(copy)
     for copy in stores:
         copy.wait()
 
@@ -588,7 +594,7 @@
             pltpu.VMEM((slots, LANES), BF16),
             pltpu.VMEM((images * patches, width), BF16),
             dma((3,)),
-            dma((width // LANES // 2 + 1,)),
+            dma((2 * (width // LANES // 2 + 1),)),
         ],
         compiler_params=pltpu.CompilerParams(vmem_limit_bytes=62 * 2**20),
     )(spread, back)

time: 65.6 us -> 65.2 us (level)
  no operation moved by 1% of the time
where the time goes in v4:
time: 65.2 us; the launch traced here: 65.1 us
  Pallas kernels  63.8 us (98%)
  between operations  1.3 us (2%)
    pallas_call x1, Pallas kernels, shards(): pl.pallas_call(exchange_kernel, out_shape=(jax.ShapeDtypeStruct((slots, k...  59.6 us
    pallas_call x1, Pallas kernels, shards(): pl.pallas_call(spread_kernel, out_shape=jax.ShapeDtypeStruct((images * pa...  4.2 us

profile of v4, /device:TPU:1, one launch (start us, length us, event | category | flops | bytes accessed | tf_op | source)
XLA Modules:
  0.0 65.1 jit_solution(881912227503433638)
XLA Ops:
  1.3 59.6 %shard_map.73 = (bf16[256,1024]{1,0:T(8,128)(2,1)}, bf16[2048,256]{1,0:T(8,128)(2,1)}) custom-call(f32[1]{0:T(128)S(6)} %copy.8.sharp_hbm, f32[1]{0:T(128)S(6)} %copy.9.shift_hbm, s32[4,96]{1,0:T(4,128)} %bitcast.8, s32[192,128]{1,0:T(8,128)} %bitcast.7, s32[768,128]{1,0:T(8,128)} %bitcast.6, bf16[384,1152]{1,0:T(8,128)(2,1)} %phrase_hbm.1, ...), custom_call_target="tpu_custom_call" | custom-call | tf_op jit(solution)/shard_map/pallas_call | solution.py:527
  60.9 4.2 %shard_map.74 = bf16[2048,1152]{1,0:T(8,128)(2,1)} custom-call(bf16[2048,256]{1,0:T(8,128)(2,1)} %get-tuple-element.7.spread_hbm, bf16[256,1024]{1,0:T(8,128)(2,1)} %get-tuple-element.8.back_hbm), custom_call_target="tpu_custom_call" | custom-call | tf_op jit(solution)/shard_map/pallas_call | solution.py:586
